TPU v7x, 32 devices: a whole 2x2x4 slice. The times are simulated.
32 devices in a mesh: grp: 4 (over z), seq: 8 (over y, x, core).
Axes of the slice: x: 2, y: 2, z: 4, core: 2. Of those that a mesh axis runs over, the one named last changes fastest.
Arguments:
- queries: bfloat16 [4096, 6144], P(('grp', 'seq')), may hold values from -64 to 64
- keys_values: bfloat16 [4096, 768], P(('grp', 'seq')), may hold values from -6 to 6
- selection: int32 [64, 32], P(('grp', 'seq')), may hold values from -1 to 63, as said below
- gate_logits: bfloat16 [3, 4096, 32], P(None, ('grp', 'seq')), may hold values from -6 to 6
- pos_weight: bfloat16 [64, 384], replicated, may hold values from -0.75 to 0.75
- compress_weight: bfloat16 [384, 384], replicated, may hold values from -0.3125 to 0.3125
Outputs:
- attended: bfloat16 [4096, 6144], P(('grp', 'seq'))
Inputs may be any that keep to these rules, and one draw needn't show every extreme that they name: `selection`: A run is the 2 rows of one device; a segment is 16 consecutive rows. Row r lists, for each group, 16 distinct block numbers no greater than r, or -1 for unused entries. Within one group, the rows of a run list from each earlier segment exactly one block, and it lies in the run at the same place of that segment; from any other run of their own segment they list at most one block.
All inputs are finite; a program needn't handle non-finite values.
Results may differ from a plain program's by a relative error of at most 0.0055.
Values may be sent and summed in bfloat16 or wider, within the bound.
A program may use at most 128 MiB of HBM per device.

v0:
```python
import math

import jax
import jax.numpy as jnp
from jax import lax
from jax.sharding import PartitionSpec as P

HEAD_DIM = 192
GROUPS = 2
GROUP_HEADS = 16
HEADS = 32
BLOCK = 64
TOP = 16
CAP = 2
WINDOW = 128


NEG_FILL = -1e30


def from_behind(block, axis, distance):
    devices = range(lax.axis_size(axis))
    route = [(i - distance, i) for i in devices if i - distance in devices]
    return lax.ppermute(block, axis, route)


def attend(query_block, key_block, allowed, with_sink):
    head_dim = query_block.shape[-1]
    score_scale = head_dim ** (-0.5)
    scores = (
        jnp.einsum(
            "btghd,bgnd->bghtn",
            query_block,
            key_block[..., :head_dim],
            preferred_element_type=jnp.float32,
        )
        * score_scale
    )
    allowed_wide = allowed[:, :, None]
    scores = jnp.where(allowed_wide, scores, NEG_FILL)
    top_score = jnp.max(scores, axis=-1, keepdims=True)
    if with_sink:
        top_score = jnp.maximum(top_score, 0.0)
    weights = jnp.where(allowed_wide, jnp.exp(scores - top_score), 0.0)
    denominator = jnp.sum(weights, axis=-1, keepdims=True)
    if with_sink:
        denominator = denominator + jnp.exp(-top_score)
    rounded = weights.astype(jnp.bfloat16)
    blended = (
        jnp.einsum(
            "bghtn,bgnd->bghtd",
            rounded,
            key_block[..., head_dim:],
            preferred_element_type=jnp.float32,
        )
        / denominator
    )
    return jnp.transpose(blended, (0, 3, 1, 2, 4))


def by_heads(query_block, key_block, allowed, with_sink):
    head_count = query_block.shape[3]
    slab_width = math.gcd(4, head_count)

    def head_slab(slab_index):
        query_slab = lax.dynamic_slice_in_dim(query_block, slab_index * slab_width, slab_width, 3)
        return attend(query_slab, key_block, allowed, with_sink)

    stacked = lax.map(head_slab, jnp.arange(head_count // slab_width, dtype=jnp.int32))
    stacked = jnp.moveaxis(stacked, 0, 3)
    return stacked.reshape(stacked.shape[:3] + (head_count, stacked.shape[-1]))


def compress_blocks(keys_values, pos_weight, compress_weight):
    block_count = keys_values.shape[0] // BLOCK
    grouped = keys_values.reshape(block_count, BLOCK, GROUPS, 2 * HEAD_DIM).astype(jnp.float32)
    pooled = jnp.sum(grouped * pos_weight.astype(jnp.float32)[None, :, None, :], axis=1).astype(
        jnp.bfloat16
    )
    mapped = jnp.dot(
        pooled.reshape(block_count * GROUPS, 2 * HEAD_DIM),
        compress_weight,
        preferred_element_type=jnp.float32,
    )
    return mapped.astype(jnp.bfloat16).reshape(block_count, GROUPS, 2 * HEAD_DIM)


def plan_requests(unit_of, key_of, wanted, unit_count, key_count):
    hits = (
        wanted[:, None, None]
        & (unit_of[:, None, None] == jnp.arange(unit_count, dtype=jnp.int32)[None, :, None])
        & (key_of[:, None, None] == jnp.arange(key_count, dtype=jnp.int32)[None, None, :])
    )
    present = jnp.any(hits, axis=0)
    ordinal = jnp.cumsum(present.astype(jnp.int32), axis=1) - 1
    slot_of = jnp.sum(jnp.where(hits, ordinal[None], 0), axis=(1, 2))
    matches = present[:, :, None] & (
        ordinal[:, :, None] == jnp.arange(CAP, dtype=jnp.int32)[None, None, :]
    )
    requests = (
        jnp.sum(
            jnp.where(matches, jnp.arange(key_count, dtype=jnp.int32)[None, :, None] + 1, 0), axis=1
        )
        - 1
    )
    return (slot_of, requests)


def shards(queries, keys_values, selection, gate_logits, pos_weight, compress_weight):
    grp_index = lax.axis_index("grp")
    seq_index = lax.axis_index("seq")
    grp_count = lax.axis_size("grp")
    seq_count = lax.axis_size("seq")
    tok_count = queries.shape[0]
    dev_blocks = tok_count // BLOCK
    seg_tokens = tok_count * seq_count
    seg_blocks = seg_tokens // BLOCK
    all_blocks = seg_blocks * grp_count
    key_count = GROUPS * dev_blocks
    first_pos = (grp_index * seq_count + seq_index) * tok_count
    positions = first_pos + jnp.arange(tok_count, dtype=jnp.int32)
    local_view = keys_values.reshape(dev_blocks, BLOCK, GROUPS, 2 * HEAD_DIM)
    local_summary = jnp.transpose(
        compress_blocks(keys_values, pos_weight, compress_weight), (1, 0, 2)
    )
    summaries = lax.all_gather(local_summary, ("grp", "seq"), axis=1, tiled=True)
    picked = selection.reshape(dev_blocks, GROUPS, TOP)
    group_ids = jnp.broadcast_to(jnp.arange(GROUPS, dtype=jnp.int32)[None, :, None], picked.shape)
    flat_groups = group_ids.reshape(-1)
    flat_picks = picked.reshape(-1)
    clipped_flat = jnp.maximum(flat_picks, 0)
    segment_of = clipped_flat // seg_blocks
    key_of = flat_groups * dev_blocks + clipped_flat % dev_blocks
    wanted = (flat_picks >= 0) & (segment_of != grp_index)
    slot_of, requests = plan_requests(segment_of, key_of, wanted, grp_count, key_count)
    asked_clipped = jnp.maximum(
        lax.all_to_all(requests, "grp", split_axis=0, concat_axis=0, tiled=True), 0
    )
    received = lax.all_to_all(
        local_view[asked_clipped % dev_blocks, :, asked_clipped // dev_blocks, :],
        "grp",
        split_axis=0,
        concat_axis=0,
        tiled=True,
    )
    picks_clipped = jnp.maximum(picked, 0)
    pick_segment = picks_clipped // seg_blocks
    from_remote = received[pick_segment, slot_of.reshape(picked.shape)]
    segment = lax.all_gather(keys_values, "seq", axis=0, tiled=True)
    earlier_tail = from_behind(segment[seg_tokens - WINDOW :], "grp", 1)
    segment_view = segment.reshape(seg_blocks, BLOCK, GROUPS, 2 * HEAD_DIM)
    from_segment = segment_view[picks_clipped % seg_blocks, :, group_ids, :]
    start_row = jnp.maximum(seq_index * tok_count - WINDOW, 0)
    inside = lax.dynamic_slice_in_dim(segment, start_row, WINDOW, 0)
    before = jnp.where(seq_index == 0, earlier_tail, inside)
    own_rows = (pick_segment == grp_index)[..., None, None]
    chosen = jnp.where(own_rows, from_segment, from_remote).reshape(
        dev_blocks, GROUPS, TOP * BLOCK, 2 * HEAD_DIM
    )
    key_positions = (picks_clipped[..., None] * BLOCK + jnp.arange(BLOCK, dtype=jnp.int32)).reshape(
        dev_blocks, GROUPS, TOP * BLOCK
    )
    live_keys = jnp.repeat(picked >= 0, BLOCK, axis=2)
    block_positions = positions.reshape(dev_blocks, BLOCK)
    allowed_sel = live_keys[:, :, None, :] & (
        key_positions[:, :, None, :] <= block_positions[:, None, :, None]
    )
    query_blocks = queries.reshape(dev_blocks, BLOCK, GROUPS, GROUP_HEADS, HEAD_DIM)
    selected_branch = by_heads(query_blocks, chosen, allowed_sel, False).reshape(
        tok_count, GROUPS, GROUP_HEADS, HEAD_DIM
    )
    query_whole = queries.reshape(1, tok_count, GROUPS, GROUP_HEADS, HEAD_DIM)
    block_ends = jnp.arange(all_blocks, dtype=jnp.int32) * BLOCK + BLOCK - 1
    allowed_comp = (block_ends[None, :] <= positions[:, None])[None, None]
    compressed_branch = by_heads(query_whole, summaries[None], allowed_comp, True)[0]
    nearby = jnp.concatenate([before, keys_values], axis=0).reshape(
        WINDOW + tok_count, GROUPS, 2 * HEAD_DIM
    )
    nearby = jnp.transpose(nearby, (1, 0, 2))[None]
    near_positions = first_pos - WINDOW + jnp.arange(WINDOW + tok_count, dtype=jnp.int32)
    allowed_win = (
        (near_positions[None, :] <= positions[:, None])
        & (near_positions[None, :] > positions[:, None] - WINDOW)
        & (near_positions[None, :] >= 0)
    )[None, None]
    window_branch = by_heads(query_whole, nearby, allowed_win, False)[0]
    gate_values = jax.nn.sigmoid(gate_logits.astype(jnp.float32)).reshape(
        3, tok_count, GROUPS, GROUP_HEADS, 1
    )
    attended = (
        gate_values[0] * compressed_branch
        + gate_values[1] * selected_branch
        + gate_values[2] * window_branch
    )
    return attended.reshape(tok_count, HEADS * HEAD_DIM).astype(jnp.bfloat16)


def solution(mesh):
    in_specs = (
        P(("grp", "seq"), None),
        P(("grp", "seq"), None),
        P(("grp", "seq"), None),
        P(None, ("grp", "seq"), None),
        P(),
        P(),
    )
    out_specs = P(("grp", "seq"), None)
    return jax.shard_map(shards, mesh=mesh, in_specs=in_specs, out_specs=out_specs, check_vma=False)
```

profile of v0, /device:TPU:0, one launch (start us, length us, event | category | flops | bytes accessed | tf_op | source)
XLA Modules:
  0.0 216.7 jit_solution(13625318544058351301)
XLA Ops:
  10.9 6.3 %all-to-all-start = ((s32[4,1,2]{2,1,0:T(1,128)}), s32[4,1,2]{2,1,0:T(1,128)}, u32[]{:S(2)}, u32[]{:S(2)}) async-start(s32[4,1,2]{2,1,0:T(1,128)} %copy.101), calls=%async_computation | async-start | bytes 4096 | tf_op jit(solution)/shard_map/all_to_all | solution.py:137
  18.9 2.6 %copy.97 = bf16[128,6144]{0,1:T(8,128)(2,1)} copy(bf16[128,6144]{1,0:T(8,128)(2,1)} %param.12) | data formatting | bytes 3145728 | tf_op args[0]
  22.0 42.4 %all_gather.6 = bf16[2,64,384]{2,0,1:T(2,128)(2,1)S(1)} all-gather(bf16[2,2,384]{2,0,1:T(2,128)(2,1)S(1)} %bitcast.261), channel_id=1, replica_groups=mesh['grp'=4,'seq'=8] {'grp','seq'}, dimensions={1}, use_global_device_ids=true | all-gather | bytes 101376 | tf_op jit(solution)/shard_map/all_gather | solution.py:126
  65.3 14.9 %while.33 = (s32[]{:T(128)}, f32[4,1,128,2,4,192]{2,5,4,0,3,1:T(8,128)S(1)}, s32[4]{0:T(128)}, bf16[1,128,2,16,192]{1,4,3,2,0:T(8,128)(2,1)}, bf16[1,2,64,384]{3...) while((s32[]{:T(128)}, ...), condition=%wide.region_4.5_spmd.clone, body=%wide.region_1.4_spmd.clone.sunk | while | flops 51128324 | bytes 2171823 | solution.py:69
  80.3 1.8 copy.106
  87.3 2.3 %gather_fusion.1 = bf16[8,64,384]{2,1,0:T(8,128)(2,1)} fusion(bf16[2,64,2,384]{3,1,2,0:T(8,128)(2,1)} %copy.106, s32[8]{0:T(128)S(1)} %reshape.547), kind=kCustom, calls=%fused_computation.1 | custom fusion | bytes 786496 | tf_op jit(solution)/shard_map/gather | solution.py:140
  89.6 3.5 %all-to-all-start.1 = ((bf16[4,2,64,384]{3,2,1,0:T(8,128)(2,1)}), bf16[4,2,64,384]{3,2,1,0:T(8,128)(2,1)S(1)}, u32[]{:S(2)}, u32[]{:S(2)}) async-start(bf16[4,2,64,384]{3,2,1,0:T(8,128)(2,1)} %bitcast.255), calls=%async_computation.1 | async-start | bytes 786432 | tf_op jit(solution)/shard_map/all_to_all | solution.py:139
  93.8 4.7 %reshape.537 = bf16[2,64,2,16,192]{4,3,2,1,0:T(8,128)(2,1)} reshape(bf16[128,6144]{1,0:T(8,128)(2,1)} %param.12) | data formatting | bytes 3145728 | tf_op jit(solution)/shard_map/reshape | solution.py:168
  99.1 6.4 %all-to-all-done.1 = bf16[4,2,64,384]{3,2,1,0:T(8,128)(2,1)S(1)} async-done(((bf16[4,2,64,384]{3,2,1,0:T(8,128)(2,1)}), bf16[4,2,64,384]{3,2,1,0:T(8,128)(2,1)S(1)}, u32[]{:S(2)}, u32[]{:S(2)}) %all-to-all-start.1) | async-done | bytes 393248 | tf_op jit(solution)/shard_map/all_to_all | solution.py:139
  105.5 2.7 %gather_fusion.2 = bf16[64,64,384]{2,1,0:T(8,128)(2,1)} fusion(bf16[4,2,64,384]{3,2,1,0:T(8,128)(2,1)S(1)} %all-to-all-done.1, s32[64]{0:T(128)S(1)} %reshape.553), kind=kCustom, calls=%fused_computation.2 | custom fusion | bytes 6291968 | tf_op jit(solution)/shard_map/gather | solution.py:148
  108.2 3.4 %reshape.538 = bf16[16,64,2,384]{3,2,1,0:T(2,128)(2,1)S(1)} reshape(bf16[1024,768]{1,0:T(8,128)(2,1)} %all-gather.2.cloned.1.call-done) | data formatting | bytes 3145728 | tf_op jit(solution)/shard_map/reshape | solution.py:151
  111.9 2.7 %gather_fusion = bf16[64,64,384]{2,1,0:T(8,128)(2,1)} fusion(bf16[16,64,2,384]{3,1,2,0:T(8,128)(2,1)S(1)} %copy.100, s32[64]{0:T(128)S(1)} %reshape.541), kind=kCustom, calls=%fused_computation | custom fusion | bytes 6291968 | tf_op jit(solution)/shard_map/gather | solution.py:152
  114.6 4.4 %broadcast_select_fusion = bf16[2,2,1024,384]{3,2,1,0:T(8,128)(2,1)} fusion(bf16[2,2,1024,384]{3,2,1,0:T(8,128)(2,1)} %bitcast.253, bf16[2,2,1024,384]{3,2,1,0:T(8,128)(2,1)} %bitcast.252, pred[2,2,1024]{2,1,0:T(4,128)(4,1)S(1)} %broadcast_in_dim.161), kind=kLoop, calls=%fused_computation.84 | loop fusion | flops 1572864 | bytes 9441280 | tf_op jit(solution)/shard_map/jit(_where)/select_n | solution.py:157
  119.0 3.2 %copy.108 = bf16[2,2,1024,384]{2,3,1,0:T(8,128)(2,1)S(1)} copy(bf16[2,2,1024,384]{3,2,1,0:T(8,128)(2,1)} %broadcast_select_fusion) | data formatting | bytes 6291456
  123.8 2.1 collective-permute-start
  125.9 30.6 %while.34 = (s32[]{:T(128)}, f32[4,2,64,2,4,192]{5,2,4,3,1,0:T(8,128)}, s32[4]{0:T(128)S(1)}, bf16[2,64,2,16,192]{4,3,2,1,0:T(8,128)(2,1)}, bf16[2,2,1024,384]{2...) while((s32[]{:T(128)}, ...), condition=%wide.region_12.13_spmd.clone, body=%wide.region_9.12_spmd.clone.sunk | while | flops 814416896 | bytes 18646196 | solution.py:69
  129.6 2.1 fusion.132
  137.3 2.1 fusion.132
  144.9 2.1 fusion.132
  147.0 1.8 fusion.133
  152.6 2.1 fusion.132
  156.4 11.7 %copy.121 = f32[2,64,2,4,4,192]{1,0,5,4,3,2:T(2,128)} copy(f32[2,64,2,4,4,192]{5,1,4,2,0,3:T(8,128)} %bitcast.16) | data formatting | bytes 6291456 | tf_op jit(solution)/shard_map/reshape;reshape | solution.py:169
  168.1 5.8 %reshape.575 = f32[128,6144]{0,1:T(8,128)S(1)} reshape(f32[2,64,2,4,4,192]{1,0,5,4,3,2:T(2,128)} %copy.121) | data formatting | bytes 6291456 | tf_op jit(solution)/shard_map/reshape;reshape | solution.py:169
  176.8 1.9 copy.111
  178.7 2.0 broadcast.656.clone2
  180.7 21.9 %while.35 = (s32[]{:T(128)}, f32[4,1,128,2,4,192]{2,5,4,0,3,1:T(8,128)}, s32[4]{0:T(128)S(1)}, bf16[1,128,2,16,192]{1,4,3,2,0:T(8,128)(2,1)}, bf16[1,2,256,384]{...) while((s32[]{:T(128)}, ...), condition=%wide.region_16.17_spmd.clone, body=%wide.region_13.16_spmd.clone.sunk | while | flops 204011520 | bytes 4873147 | solution.py:69
  184.0 2.2 %fusion.138 = f32[4,1,128,2,4,192]{2,5,4,0,3,1:T(8,128)} fusion(f32[4,1,128,2,4,192]{2,5,4,0,3,1:T(8,128)} %get-tuple-element.488, s32[]{:T(128)} %get-tuple-element.487, f32[1,2,4,128,256]{4,3,2,1,0:T(8,128)S(1)} %get-tuple-element.472, f32[2,4,128]{2,1,0:T(4,128)S(1)} %get-tuple-element.473, pred[128,256]{1,0:T(8,128)(4,1)S(1)} %and_and_fusion.2, ...), kind=kOutput, calls=%fused_computation.60.clone.1 | convolution fusion | flops 101646336 | bytes 2073088 | tf_op jit(solution)/shard_map/while/body/eval_jaxpr/bghtn,bgnd->bghtd/dot_general | solution.py:50
  189.4 2.2 %fusion.138 = f32[4,1,128,2,4,192]{2,5,4,0,3,1:T(8,128)} fusion(f32[4,1,128,2,4,192]{2,5,4,0,3,1:T(8,128)} %get-tuple-element.488, s32[]{:T(128)} %get-tuple-element.487, f32[1,2,4,128,256]{4,3,2,1,0:T(8,128)S(1)} %get-tuple-element.472, f32[2,4,128]{2,1,0:T(4,128)S(1)} %get-tuple-element.473, pred[128,256]{1,0:T(8,128)(4,1)S(1)} %and_and_fusion.2, ...), kind=kOutput, calls=%fused_computation.60.clone.1 | convolution fusion | flops 101646336 | bytes 2073088 | tf_op jit(solution)/shard_map/while/body/eval_jaxpr/bghtn,bgnd->bghtd/dot_general | solution.py:50
  194.9 2.2 %fusion.138 = f32[4,1,128,2,4,192]{2,5,4,0,3,1:T(8,128)} fusion(f32[4,1,128,2,4,192]{2,5,4,0,3,1:T(8,128)} %get-tuple-element.488, s32[]{:T(128)} %get-tuple-element.487, f32[1,2,4,128,256]{4,3,2,1,0:T(8,128)S(1)} %get-tuple-element.472, f32[2,4,128]{2,1,0:T(4,128)S(1)} %get-tuple-element.473, pred[128,256]{1,0:T(8,128)(4,1)S(1)} %and_and_fusion.2, ...), kind=kOutput, calls=%fused_computation.60.clone.1 | convolution fusion | flops 101646336 | bytes 2073088 | tf_op jit(solution)/shard_map/while/body/eval_jaxpr/bghtn,bgnd->bghtd/dot_general | solution.py:50
  200.4 2.3 %fusion.138 = f32[4,1,128,2,4,192]{2,5,4,0,3,1:T(8,128)} fusion(f32[4,1,128,2,4,192]{2,5,4,0,3,1:T(8,128)} %get-tuple-element.488, s32[]{:T(128)} %get-tuple-element.487, f32[1,2,4,128,256]{4,3,2,1,0:T(8,128)S(1)} %get-tuple-element.472, f32[2,4,128]{2,1,0:T(4,128)S(1)} %get-tuple-element.473, pred[128,256]{1,0:T(8,128)(4,1)S(1)} %and_and_fusion.2, ...), kind=kOutput, calls=%fused_computation.60.clone.1 | convolution fusion | flops 101646336 | bytes 2073088 | tf_op jit(solution)/shard_map/while/body/eval_jaxpr/bghtn,bgnd->bghtd/dot_general | solution.py:50
  202.6 4.6 %fusion.84 = bf16[128,6144]{0,1:T(8,128)(2,1)} fusion(f32[4,1,128,2,4,192]{2,5,4,0,3,1:T(8,128)} %get-tuple-element.103, f32[4,1,128,2,4,192]{2,5,4,0,3,1:T(8,128)} %copy-done.1, f32[128,6144]{0,1:T(8,128)S(1)} %reshape.575, f32[128,2,16]{0,2,1:T(8,128)S(1)} %bitcast.259, f32[128,2,16]{0,2,1:T(8,128)S(1)} %bitcast.260, f32[128,2,16]{0,2,1:T(8,128)S(1)} %bitcast.258), kind=kLoop, calls=%fused_computation.80 | loop fusion | flops 4718592 | bytes 11059200 | tf_op jit(solution)/shard_map/convert_element_type | solution.py:195
  207.3 2.6 %copy.113 = bf16[128,6144]{1,0:T(8,128)(2,1)} copy(bf16[128,6144]{0,1:T(8,128)(2,1)} %fusion.84) | data formatting | bytes 3145728 | tf_op jit(solution)/shard_map/convert_element_type | solution.py:195
  (155 shorter events, 58.9 us)
Async XLA Ops:
  6.5 15.3 %copy-start = (bf16[384,384]{1,0:T(8,128)(2,1)S(1)}, bf16[384,384]{1,0:T(8,128)(2,1)}, u32[]{:S(2)}) copy-start(bf16[384,384]{1,0:T(8,128)(2,1)} %param.17) | copy-start | bytes 884740
  6.5 15.0 %copy-start.3 = (bf16[64,384]{1,0:T(8,128)(2,1)S(1)}, bf16[64,384]{1,0:T(8,128)(2,1)}, u32[]{:S(2)}) copy-start(bf16[64,384]{1,0:T(8,128)(2,1)} %param.16) | copy-start | bytes 147460
  9.1 8.1 %copy-start.7 = (pred[2,32]{1,0:T(4,128)(4,1)}, pred[2,32]{1,0:T(4,128)(4,1)S(1)}, u32[]{:S(2)}) copy-start(pred[2,32]{1,0:T(4,128)(4,1)S(1)} %get-tuple-element.310) | copy-start | bytes 196
  9.1 8.1 %copy-start.8 = (pred[2,32]{1,0:T(4,128)(4,1)}, pred[2,32]{1,0:T(4,128)(4,1)S(1)}, u32[]{:S(2)}) copy-start(pred[2,32]{1,0:T(4,128)(4,1)S(1)} %get-tuple-element.293) | copy-start | bytes 196
  9.5 0.5 copy-start.5
  9.5 12.5 %copy-start.6 = (pred[64,4]{0,1:T(4,128)(4,1)}, pred[64,4]{0,1:T(4,128)(4,1)S(1)}, u32[]{:S(2)}) copy-start(pred[64,4]{0,1:T(4,128)(4,1)S(1)} %get-tuple-element.312) | copy-start | bytes 772
  10.9 75.5 %all-to-all-start = ((s32[4,1,2]{2,1,0:T(1,128)}), s32[4,1,2]{2,1,0:T(1,128)}, u32[]{:S(2)}, u32[]{:S(2)}) async-start(s32[4,1,2]{2,1,0:T(1,128)} %copy.101), calls=%async_computation | async-start | bytes 4096 | tf_op jit(solution)/shard_map/all_to_all | solution.py:137
  17.2 91.0 %all-gather.2.cloned.1.call-start = ((), (), s32[]{:S(2)}) async-start(), calls=%async_computation.2 | async-start | bytes 1769472 | tf_op jit(solution)/shard_map/all_gather | solution.py:149
  18.9 45.5 %copy-start.2 = (bf16[2,64,2,384]{3,2,1,0:T(2,128)(2,1)}, bf16[2,64,2,384]{3,2,1,0:T(2,128)(2,1)S(1)}, u32[]{:S(2)}) copy-start(bf16[2,64,2,384]{3,2,1,0:T(2,128)(2,1)S(1)} %reshape.535) | copy-start | bytes 589828
  80.2 9.4 %copy-start.1 = (f32[4,1,128,2,4,192]{2,5,4,0,3,1:T(8,128)}, f32[4,1,128,2,4,192]{2,5,4,0,3,1:T(8,128)S(1)}, u32[]{:S(2)}) copy-start(f32[4,1,128,2,4,192]{2,5,4,0,3,1:T(8,128)S(1)} %get-tuple-element.101) | copy-start | bytes 9437188
  80.2 18.9 %copy-start.4 = (bf16[3,128,32]{1,2,0:T(8,128)(2,1)S(1)}, bf16[3,128,32]{1,2,0:T(8,128)(2,1)}, u32[]{:S(2)}) copy-start(bf16[3,128,32]{1,2,0:T(8,128)(2,1)} %param.15) | copy-start | bytes 73732
  89.6 15.9 %all-to-all-start.1 = ((bf16[4,2,64,384]{3,2,1,0:T(8,128)(2,1)}), bf16[4,2,64,384]{3,2,1,0:T(8,128)(2,1)S(1)}, u32[]{:S(2)}, u32[]{:S(2)}) async-start(bf16[4,2,64,384]{3,2,1,0:T(8,128)(2,1)} %bitcast.255), calls=%async_computation.1 | async-start | bytes 786432 | tf_op jit(solution)/shard_map/all_to_all | solution.py:139
  123.8 50.2 %collective-permute-start = (bf16[128,768]{1,0:T(8,128)(2,1)}, bf16[128,768]{1,0:T(8,128)(2,1)}, u32[]{:S(2)}, u32[]{:S(2)}) collective-permute-start(bf16[128,768]{1,0:T(8,128)(2,1)} %slice.52), channel_id=1, source_target_pairs={{0,8},{8,16},{16,24},{1,9},{9,17},{17,25},{2,10},{10,18},{18,26},{... | collective-permute-start | bytes 589832 | tf_op jit(solution)/shard_map/ppermute | solution.py:24
Sparse Core Ops, SparseCore 0:
  19.9 27.4 all-gather.1
where the time goes:
time: 218 us; the launch traced here: 217 us
  local copies, waits for them, and re-layouts  74.2 us (34%)
  blocking collectives  42.4 us (19%)
  matrix products  31.7 us (15%)
  other arithmetic  28.2 us (13%)
  between operations  13.7 us (6%)
  starting transfers between devices  11.9 us (5%)
  loops' own time  7.63 us (4%)
  waiting for transfers between devices  7.09 us (3%)
    all_gather x1, blocking collectives, shards(): lax.all_gather(local_summary, ('grp', 'seq'), axis=1, tiled=True)  42.4 us
    dot_general x12, matrix products, attend(): jnp.einsum('bghtn,bgnd->bghtd', rounded, key_block[..., head_dim:], prefe...  17.7 us
    another operation x2, local copies, waits for them, and re-layouts, shards(): by_heads(query_blocks, chosen, allowed_sel, False)  17.5 us
    dot_general x12, matrix products, attend(): jnp.einsum('btghd,bgnd->bghtn', query_block, key_block[..., :head_dim], p...  13.8 us
    dynamic_slice x12, local copies, waits for them, and re-layouts, by_heads(): lax.map(head_slab, jnp.arange(head_count // slab_width, dtype=jnp.int32))  9.99 us
    sub x4, other arithmetic, attend(): weights = jnp.where(allowed_wide, jnp.exp(scores - top_score), 0.0)  8.59 us
    another operation x3, loops' own time, by_heads(): lax.map(head_slab, jnp.arange(head_count // slab_width, dtype=jnp.int32))  7.63 us
    all_to_all x1, waiting for transfers between devices, shards(): lax.all_to_all(local_view[asked_clipped % dev_blocks, :, asked_clipped //...  6.38 us
  transfers between devices with their start and end apart: 4, of which 1 were waited for; matrix products, arithmetic and copies ran while one was open for 37% of the time, Pallas kernels for 0%

commit v1 on v0

v1 whole, which is shorter than its diff:
```python
import functools
import math

import jax
import jax.numpy as jnp
from jax import lax
from jax.experimental import pallas as pl
from jax.experimental.pallas import tpu as pltpu
from jax.sharding import PartitionSpec as P

HEAD_DIM = 192
GROUPS = 2
GROUP_HEADS = 16
HEADS = 32
BLOCK = 64
TOP = 16
WINDOW = 128
PAIR = 2 * HEAD_DIM
WIDE = 256
CHUNK = 4
PAIRS = GROUP_HEADS // 2
NEG_FILL = -1e30
EXP2_SCALE = HEAD_DIM ** (-0.5) * math.log2(math.e)
FAR_POS = 1 << 30


def exchange(grp_count, seq_count, kv_ref, sel_ref, pos_ref, map_ref, pool_ref, prev_ref, sums_ref,
             lists, staged, mine, list_send, list_recv, data_send, data_recv, sum_send, sum_recv,
             prev_send, prev_recv):
    grp = lax.axis_index("grp")
    seq = lax.axis_index("seq")
    last = seq_count - 1
    first_block = (grp * seq_count + seq) * 2

    barrier = pltpu.get_barrier_semaphore()

    def near(place):
        return (grp, place)

    def far(segment):
        return (segment, seq)

    def greet(where):
        pl.semaphore_signal(barrier, inc=1, device_id=where, device_id_type=pl.DeviceIdType.MESH)

    def each(low, high, body):
        def step(i, carry):
            body(i)
            return carry

        lax.fori_loop(low, high, step, 0)

    def others(count, me, body):
        each(0, me, body)
        each(me + 1, count, body)

    others(seq_count, seq, lambda i: greet(near(i)))
    others(grp_count, grp, lambda i: greet(far(i)))
    tail_out = jnp.logical_and(seq == last, grp < grp_count - 1)
    tail_in = jnp.logical_and(seq == 0, grp > 0)

    @pl.when(tail_out)
    def _():
        greet((grp + 1, 0))

    @pl.when(tail_in)
    def _():
        greet((grp - 1, last))

    extra = tail_out.astype(jnp.int32) + tail_in.astype(jnp.int32)
    pl.semaphore_wait(barrier, seq_count + grp_count - 2 + extra)

    def remote(src, dst, send, recv, where):
        return pltpu.make_async_remote_copy(
            src_ref=src, dst_ref=dst, send_sem=send, recv_sem=recv, device_id=where,
            device_id_type=pl.DeviceIdType.MESH)

    def list_copy(theirs, own, where):
        return remote(sel_ref, lists.at[own], list_send.at[theirs], list_recv.at[own], where)

    each(0, grp, lambda i: list_copy(seq_count + i, seq_count + grp, far(i)).start())
    each(0, seq, lambda i: list_copy(i, seq, near(i)).start())

    def prev_copy(where):
        return remote(kv_ref, prev_ref, prev_send, prev_recv, where)

    @pl.when(seq < last)
    def _():
        prev_copy((grp, seq + 1)).start()

    @pl.when(tail_out)
    def _():
        prev_copy((grp + 1, 0)).start()

    rows = []
    for b in range(2):
        for g in range(GROUPS):
            part = kv_ref[b * BLOCK:(b + 1) * BLOCK, g * PAIR:(g + 1) * PAIR].astype(jnp.float32)
            rows.append(jnp.sum(part * pos_ref[...].astype(jnp.float32), axis=0, keepdims=True))
    pooled = jnp.concatenate(rows + [jnp.zeros((4, PAIR), jnp.float32)], axis=0).astype(jnp.bfloat16)
    mapped = jnp.dot(pooled, map_ref[...], preferred_element_type=jnp.float32)
    packed = jnp.concatenate(
        [mapped[0:4, c * 128:(c + 1) * 128] for c in range(3)] + [jnp.zeros((4, 128), jnp.float32)], axis=0)
    mine[...] = packed.astype(jnp.bfloat16)
    sums_ref[seq, grp] = mine[...]

    def column_copy(theirs, own, where):
        return remote(mine, sums_ref.at[seq, grp], sum_send.at[theirs], sum_recv.at[own], where)

    others(grp_count, grp, lambda i: column_copy(seq_count + i, seq_count + grp, far(i)).start())

    def data_copy(theirs, own, where):
        return remote(staged.at[theirs], pool_ref.at[own], data_send.at[theirs], data_recv.at[own], where)

    def answer(slot, own, where):
        list_copy(slot, slot, where).wait_recv()
        hit = jnp.where(lists[slot] == first_block + 1, 1.0, 0.0)
        for g in range(GROUPS):
            second = jnp.max(hit[:, g * TOP:(g + 1) * TOP], axis=(0, 1), keepdims=True)
            cols = pl.ds(g * PAIR, PAIR)
            low = kv_ref[0:BLOCK, cols].astype(jnp.float32)
            high = kv_ref[BLOCK:2 * BLOCK, cols].astype(jnp.float32)
            pick = jnp.broadcast_to(second, (BLOCK, PAIR)) > 0.5
            staged[slot, :, cols] = jnp.where(pick, high, low).astype(jnp.bfloat16)
        data_copy(slot, own, where).start()

    each(grp + 1, grp_count, lambda i: answer(seq_count + i, seq_count + grp, far(i)))
    each(seq + 1, seq_count, lambda i: answer(i, seq, near(i)))

    others(grp_count, grp, lambda i: column_copy(seq_count + i, seq_count + i, far(i)).wait_recv())

    def row_copy(theirs, own, where):
        return remote(sums_ref.at[seq], sums_ref.at[own], sum_send.at[theirs], sum_recv.at[own], where)

    others(seq_count, seq, lambda i: row_copy(i, seq, near(i)).start())

    def row_wait(i):
        remote(sums_ref.at[seq], sums_ref.at[i], sum_send.at[i], sum_recv.at[i], near(i)).wait_recv()

    others(seq_count, seq, row_wait)

    each(0, grp, lambda i: data_copy(seq_count + i, seq_count + i, far(i)).wait_recv())
    each(0, seq, lambda i: data_copy(i, i, near(i)).wait_recv())

    @pl.when(jnp.logical_or(seq > 0, grp > 0))
    def _():
        prev_copy(far(grp)).wait_recv()

    @pl.when(jnp.logical_or(seq < last, grp < grp_count - 1))
    def _():
        prev_copy(far(grp)).wait_send()

    each(0, grp, lambda i: list_copy(seq_count + i, seq_count + i, far(i)).wait_send())
    each(0, seq, lambda i: list_copy(i, i, near(i)).wait_send())
    each(grp + 1, grp_count, lambda i: data_copy(seq_count + i, seq_count + i, far(i)).wait_send())
    each(seq + 1, seq_count, lambda i: data_copy(i, i, near(i)).wait_send())
    others(grp_count, grp, lambda i: column_copy(seq_count + i, seq_count + i, far(i)).wait_send())
    others(seq_count, seq, lambda i: row_copy(i, seq, near(i)).wait_send())


def run_exchange(keys_values, selection, pos_weight, compress_weight):
    grp_count = lax.axis_size("grp")
    seq_count = lax.axis_size("seq")
    slots = grp_count + seq_count
    vmem = pl.BlockSpec(memory_space=pltpu.VMEM)
    dma = pltpu.SemaphoreType.DMA((slots,))
    return pl.pallas_call(
        functools.partial(exchange, grp_count, seq_count),
        out_shape=(
            jax.ShapeDtypeStruct((slots, BLOCK, GROUPS * PAIR), jnp.bfloat16),
            jax.ShapeDtypeStruct(keys_values.shape, jnp.bfloat16),
            jax.ShapeDtypeStruct((seq_count, grp_count, 16, 128), jnp.bfloat16),
        ),
        in_specs=[vmem] * 4,
        out_specs=(pl.BlockSpec(memory_space=pl.ANY), pl.BlockSpec(memory_space=pl.ANY), vmem),
        scratch_shapes=[
            pltpu.VMEM((slots,) + selection.shape, jnp.int32),
            pltpu.VMEM((slots, BLOCK, GROUPS * PAIR), jnp.bfloat16),
            pltpu.VMEM((16, 128), jnp.bfloat16),
            dma, dma, dma, dma, dma, dma,
            pltpu.SemaphoreType.DMA,
            pltpu.SemaphoreType.DMA,
        ],
        compiler_params=pltpu.CompilerParams(
            collective_id=0, has_side_effects=True, vmem_limit_bytes=32 << 20),
    )(keys_values, selection, pos_weight, compress_weight)


def spread(pair):
    lane = lax.broadcasted_iota(jnp.int32, (pair.shape[0], WIDE), 1)
    low = pair[:, 0:WIDE].astype(jnp.float32)
    high = pair[:, PAIR - WIDE:PAIR].astype(jnp.float32)
    key_even = jnp.where(lane < HEAD_DIM, low, 0.0)
    key_odd = jnp.where(lane >= WIDE - HEAD_DIM, pltpu.roll(low, WIDE - HEAD_DIM, 1), 0.0)
    value_even = jnp.where(lane < HEAD_DIM, pltpu.roll(high, HEAD_DIM, 1),
                           jnp.where(lane == HEAD_DIM, 1.0, 0.0))
    value_odd = jnp.where(lane >= WIDE - HEAD_DIM, high, jnp.where(lane == 0, 1.0, 0.0))
    return [x.astype(jnp.bfloat16) for x in (key_even, key_odd, value_even, value_odd)]


def branch(query_rows, keys, values, biases, with_sink, ones_lane):
    heads = query_rows.shape[0] // BLOCK
    scores = []
    for key, bias in zip(keys, biases):
        raw = lax.dot_general(query_rows, key, (((1,), (1,)), ((), ())), preferred_element_type=jnp.float32)
        scores.append((raw.reshape(heads, BLOCK, raw.shape[1]) + bias[None]).reshape(raw.shape))
    top = functools.reduce(jnp.maximum, [jnp.max(s, axis=1, keepdims=True) for s in scores])
    if with_sink:
        top = jnp.maximum(top, 0.0)
    total = None
    for score, value in zip(scores, values):
        weights = jnp.exp2((score - top) * EXP2_SCALE).astype(jnp.bfloat16)
        part = jnp.dot(weights, value, preferred_element_type=jnp.float32)
        total = part if total is None else total + part
    below = total[:, ones_lane:ones_lane + 1]
    if with_sink:
        below = below + jnp.exp2(-top * EXP2_SCALE)
    return total, below


def attend(grp_count, seq_count, sel_ref, q_ref, kv_ref, pool_ref, prev_ref, sums_ref, gate_ref,
           out_ref, chosen, nearby, far_sums, acc, picks, spots):
    slots = grp_count + seq_count
    grp = lax.axis_index("grp")
    seq = lax.axis_index("seq")
    g = pl.program_id(0)
    b = pl.program_id(1)
    run = grp * seq_count + seq
    row_block = run * 2 + b
    cols = pl.ds(pl.multiple_of(g * PAIR, 128), PAIR)
    halves = PAIRS // 4

    @pl.when(b == 0)
    def _():
        def fill(slot, carry):
            for i, x in enumerate(spread(pool_ref[slot, :, cols])):
                chosen[i, slot] = x
            return carry

        lax.fori_loop(0, seq, fill, 0)
        lax.fori_loop(seq_count, seq_count + grp, fill, 0)
        own = spread(kv_ref[:, cols])
        before = spread(jnp.where(run > 0, prev_ref[:, cols], jnp.zeros_like(prev_ref[:, cols])))
        for i in range(4):
            chosen[i, slots] = own[i][0:BLOCK]
            chosen[i, slots + 1] = own[i][BLOCK:2 * BLOCK]
            nearby[i, 0:WINDOW] = before[i]
            nearby[i, WINDOW:2 * WINDOW] = own[i]
        for i, x in enumerate(spread(sums_ref[0])):
            far_sums[i] = x

    seg_blocks = 2 * seq_count

    def scan(i, count):
        block = sel_ref[b, g * TOP + i]
        segment = block // seg_blocks
        place = (block - segment * seg_blocks) // 2
        here = jnp.logical_and(segment == grp, place == seq)
        slot = jnp.where(here, slots + (block & 1), jnp.where(segment == grp, place, seq_count + segment))

        @pl.when(block >= 0)
        def _():
            picks[count] = slot
            spots[count] = block * BLOCK

        return count + jnp.where(block >= 0, 1, 0)

    for i in range(TOP):
        picks[i] = slots + b
        spots[i] = FAR_POS
    count = lax.fori_loop(0, TOP, scan, jnp.int32(0))

    @pl.when(count < TOP)
    def _():
        def blank(i, carry):
            picks[i] = slots + b
            spots[i] = FAR_POS
            return carry

        lax.fori_loop(count, TOP, blank, 0)

    token = row_block * BLOCK + lax.broadcasted_iota(jnp.int32, (BLOCK, 1), 0)

    def bias_of(allowed):
        return jnp.where(allowed, 0.0, NEG_FILL)

    key_pos = run * 2 * BLOCK - WINDOW + lax.broadcasted_iota(jnp.int32, (BLOCK, 2 * WINDOW), 1)
    near_bias = bias_of((key_pos <= token) & (key_pos > token - WINDOW) & (key_pos >= 0))
    all_blocks = sums_ref.shape[1]
    block_end = lax.broadcasted_iota(jnp.int32, (BLOCK, all_blocks), 1) * BLOCK + BLOCK - 1
    sums_bias = bias_of(block_end <= token)

    gates = []
    for i in range(3):
        full = 1.0 / (1.0 + jnp.exp(-gate_ref[i].astype(jnp.float32)))
        gates.append(jnp.where(g == 0, full[:, 0:GROUP_HEADS], full[:, GROUP_HEADS:HEADS]))

    def rows_of(half, parity):
        starts = [(half * 4 + j) * PAIR + parity * (PAIR - WIDE) for j in range(4)]
        return jnp.concatenate([q_ref[:, s:s + WIDE] for s in starts], axis=0)

    def gate_of(i, half, parity):
        heads = [2 * (half * 4 + j) + parity for j in range(4)]
        return jnp.concatenate([gates[i][:, h:h + 1] for h in heads], axis=0)

    ones_lane = (HEAD_DIM, 0)
    for half in range(halves):
        for parity in range(2):
            rows = rows_of(half, parity)
            near_total, near_below = branch(
                rows, [nearby[parity]], [nearby[2 + parity]], [near_bias], False, ones_lane[parity])
            sums_total, sums_below = branch(
                rows, [far_sums[parity]], [far_sums[2 + parity]], [sums_bias], True, ones_lane[parity])
            acc[half, parity] = (near_total * (gate_of(2, half, parity) / near_below)
                                 + sums_total * (gate_of(0, half, parity) / sums_below))

    lane = lax.broadcasted_iota(jnp.int32, (BLOCK, CHUNK * BLOCK), 1)
    half_lane = lax.broadcasted_iota(jnp.int32, (BLOCK, 128), 1) < 64

    def selected(chunks):
        biases = []
        for c in range(chunks):
            base = jnp.full(lane.shape, spots[c * CHUNK], jnp.int32)
            for j in range(1, CHUNK):
                base = jnp.where(lane >= j * BLOCK, spots[c * CHUNK + j], base)
            biases.append(bias_of(base + (lane & (BLOCK - 1)) <= token))
        for half in range(halves):
            both = []
            for parity in range(2):
                def take(which):
                    return [
                        jnp.concatenate([chosen[which, picks[c * CHUNK + j]] for j in range(CHUNK)], axis=0)
                        for c in range(chunks)
                    ]

                total, below = branch(
                    rows_of(half, parity), take(parity), take(2 + parity), biases, False, ones_lane[parity])
                both.append(acc[half, parity] + total * (gate_of(1, half, parity) / below))
            for j in range(4):
                even = both[0][j * BLOCK:(j + 1) * BLOCK]
                odd = both[1][j * BLOCK:(j + 1) * BLOCK]
                start = (half * 4 + j) * PAIR
                out_ref[:, start:start + 128] = even[:, 0:128].astype(jnp.bfloat16)
                out_ref[:, start + 128:start + 256] = jnp.where(
                    half_lane, even[:, 128:256], odd[:, 0:128]).astype(jnp.bfloat16)
                out_ref[:, start + 256:start + 384] = odd[:, 128:256].astype(jnp.bfloat16)

    for chunks in range(1, TOP // CHUNK + 1):
        low = 0 if chunks == 1 else (chunks - 1) * CHUNK + 1

        @pl.when(jnp.logical_and(count >= low, count <= chunks * CHUNK))
        def _():
            selected(chunks)


def run_attend(selection, queries, keys_values, pool, prev, sums, gate_logits):
    grp_count = lax.axis_size("grp")
    seq_count = lax.axis_size("seq")
    slots = grp_count + seq_count
    all_blocks = sums.shape[1]

    def whole(x):
        return pl.BlockSpec(x.shape, lambda g, b, *_: (0,) * x.ndim)

    group_cols = GROUP_HEADS * HEAD_DIM
    return pl.pallas_call(
        functools.partial(attend, grp_count, seq_count),
        out_shape=jax.ShapeDtypeStruct(queries.shape, jnp.bfloat16),
        grid_spec=pltpu.PrefetchScalarGridSpec(
            num_scalar_prefetch=1,
            grid=(GROUPS, 2),
            in_specs=[
                pl.BlockSpec((BLOCK, group_cols), lambda g, b, *_: (b, g)),
                whole(keys_values), whole(pool), whole(prev),
                pl.BlockSpec((1, all_blocks, PAIR), lambda g, b, *_: (g, 0, 0)),
                pl.BlockSpec((3, BLOCK, HEADS), lambda g, b, *_: (0, b, 0)),
            ],
            out_specs=pl.BlockSpec((BLOCK, group_cols), lambda g, b, *_: (b, g)),
            scratch_shapes=[
                pltpu.VMEM((4, slots + 2, BLOCK, WIDE), jnp.bfloat16),
                pltpu.VMEM((4, 2 * WINDOW, WIDE), jnp.bfloat16),
                pltpu.VMEM((4, all_blocks, WIDE), jnp.bfloat16),
                pltpu.VMEM((PAIRS // 4, 2, 4 * BLOCK, WIDE), jnp.float32),
                pltpu.SMEM((TOP,), jnp.int32),
                pltpu.SMEM((TOP,), jnp.int32),
            ],
        ),
        compiler_params=pltpu.CompilerParams(vmem_limit_bytes=48 << 20),
    )(selection, queries, keys_values, pool, prev, sums, gate_logits)


def shards(queries, keys_values, selection, gate_logits, pos_weight, compress_weight):
    grp_count = lax.axis_size("grp")
    seq_count = lax.axis_size("seq")
    pool, prev, packed = run_exchange(keys_values, selection, pos_weight, compress_weight)
    sums = packed[:, :, :12].reshape(seq_count, grp_count, 3, 2, GROUPS, 128)
    sums = jnp.transpose(sums, (4, 1, 0, 3, 2, 5)).reshape(GROUPS, 2 * seq_count * grp_count, PAIR)
    return run_attend(selection, queries, keys_values, pool, prev, sums, gate_logits)


def solution(mesh):
    in_specs = (
        P(("grp", "seq"), None),
        P(("grp", "seq"), None),
        P(("grp", "seq"), None),
        P(None, ("grp", "seq"), None),
        P(),
        P(),
    )
    out_specs = P(("grp", "seq"), None)
    return jax.shard_map(shards, mesh=mesh, in_specs=in_specs, out_specs=out_specs, check_vma=False)
```

time: 218 us -> 50.7 us (0.23)
  the two profiles are of different devices: /device:TPU:0 before, /device:TPU:7 now
where the time goes in v1:
time: 50.7 us; the launch traced here: 50.3 us
  Pallas kernels  42.8 us (84%)
  local copies, waits for them, and re-layouts  7.44 us (15%)
    pallas_call x1, Pallas kernels, run_attend(): pl.pallas_call(functools.partial(attend, grp_count, seq_count), out_shape...  23.5 us
    pallas_call x1, Pallas kernels, run_exchange(): pl.pallas_call(functools.partial(exchange, grp_count, seq_count), out_sha...  19.3 us
    unnamed x15, local copies, waits for them, and re-layouts  7.22 us

profile of v1, /device:TPU:7, one launch (start us, length us, event | category | flops | bytes accessed | tf_op | source)
XLA Modules:
  0.0 50.3 jit_solution(18150152973223662922)
XLA Ops:
  0.0 0.9 %copy.11.gate_ref = bf16[3,128,32]{2,1,0:T(8,128)(2,1)S(1)} copy(bf16[3,128,32]{1,2,0:T(8,128)(2,1)} %param.9) | data formatting | bytes 49152 | tf_op args[3]
  0.9 0.0 copy-start.1
  0.9 0.9 %copy-done.1 = bf16[128,768]{1,0:T(8,128)(2,1)S(1)} copy-done((bf16[128,768]{1,0:T(8,128)(2,1)S(1)}, bf16[128,768]{1,0:T(8,128)(2,1)}, u32[]{:S(2)}) %copy-start.1) | copy-done | bytes 196632
  1.8 0.0 copy-start.3
  1.8 1.0 %copy-done.3 = bf16[384,384]{1,0:T(8,128)(2,1)S(1)} copy-done((bf16[384,384]{1,0:T(8,128)(2,1)S(1)}, bf16[384,384]{1,0:T(8,128)(2,1)}, u32[]{:S(2)}) %copy-start.3) | copy-done | bytes 294936
  2.7 0.0 copy-start.4
  2.8 0.8 %copy-done.4 = bf16[64,384]{1,0:T(8,128)(2,1)S(1)} copy-done((bf16[64,384]{1,0:T(8,128)(2,1)S(1)}, bf16[64,384]{1,0:T(8,128)(2,1)}, u32[]{:S(2)}) %copy-start.4) | copy-done | bytes 49176
  3.5 0.0 copy-start.5
  3.6 0.7 %copy-done.5 = s32[2,32]{1,0:T(2,128)S(1)} copy-done((s32[2,32]{1,0:T(2,128)S(1)}, s32[2,32]{1,0:T(2,128)}, u32[]{:S(2)}) %copy-start.5) | copy-done | bytes 280
  4.2 19.3 %shard_map.64 = (bf16[12,64,768]{2,1,0:T(8,128)(2,1)S(1)}, bf16[128,768]{1,0:T(8,128)(2,1)S(1)}, bf16[8,4,16,128]{3,2,1,0:T(8,128)(2,1)S(1)}) custom-call(bf16[128,768]{1,0:T(8,128)(2,1)S(1)} %copy-done.1, s32[2,32]{1,0:T(2,128)S(1)} %copy-done.5, bf16[64,384]{1,0:T(8,128)(2,1)S(1)} %copy-done.4, bf16[384,384]{1,0:T(8,128)(2,1)S(1)} %copy-done.3), custom_call_target="tpu_custom_call" | custom-call | tf_op jit(solution)/shard_map/pallas_call | solution.py:167
  23.5 0.1 copy.9
  23.6 0.1 copy.10
  23.7 0.1 reshape.7.sums_ref
  23.8 0.0 copy-start
  23.8 1.4 %copy-done = bf16[128,6144]{1,0:T(8,128)(2,1)S(1)} copy-done((bf16[128,6144]{1,0:T(8,128)(2,1)S(1)}, bf16[128,6144]{1,0:T(8,128)(2,1)}, u32[]{:S(2)}) %copy-start) | copy-done | bytes 1572888
  25.2 0.0 copy-start.2
  25.2 0.9 %copy-done.2 = bf16[128,768]{1,0:T(8,128)(2,1)S(1)} copy-done((bf16[128,768]{1,0:T(8,128)(2,1)S(1)}, bf16[128,768]{1,0:T(8,128)(2,1)}, u32[]{:S(2)}) %copy-start.2) | copy-done | bytes 196632
  26.1 0.0 copy-start.6
  26.1 0.7 %copy-done.6 = s32[2,32]{1,0:T(2,128)S(1)} copy-done((s32[2,32]{1,0:T(2,128)S(1)}, s32[2,32]{1,0:T(2,128)}, u32[]{:S(2)}) %copy-start.6) | copy-done | bytes 280
  26.8 23.5 %shard_map.65 = bf16[128,6144]{1,0:T(8,128)(2,1)} custom-call(s32[2,32]{1,0:T(2,128)S(1)} %copy-done.6, bf16[128,6144]{1,0:T(8,128)(2,1)S(1)} %copy-done, bf16[128,768]{1,0:T(8,128)(2,1)S(1)} %copy-done.2, bf16[12,64,768]{2,1,0:T(8,128)(2,1)S(1)} %get-tuple-element.8.pool_ref, bf16[128,768]{1,0:T(8,128)(2,1)S(1)} %get-tuple-element.9.prev_ref, ...), custom_call_target="tpu_custom_call" | custom-call | tf_op jit(solution)/shard_map/pallas_call | solution.py:366
Async XLA Ops:
  0.9 0.9 %copy-start.1 = (bf16[128,768]{1,0:T(8,128)(2,1)S(1)}, bf16[128,768]{1,0:T(8,128)(2,1)}, u32[]{:S(2)}) copy-start(bf16[128,768]{1,0:T(8,128)(2,1)} %kv_ref.3) | copy-start | bytes 589828
  1.8 1.0 %copy-start.3 = (bf16[384,384]{1,0:T(8,128)(2,1)S(1)}, bf16[384,384]{1,0:T(8,128)(2,1)}, u32[]{:S(2)}) copy-start(bf16[384,384]{1,0:T(8,128)(2,1)} %map_ref.1) | copy-start | bytes 884740
  2.7 0.8 %copy-start.4 = (bf16[64,384]{1,0:T(8,128)(2,1)S(1)}, bf16[64,384]{1,0:T(8,128)(2,1)}, u32[]{:S(2)}) copy-start(bf16[64,384]{1,0:T(8,128)(2,1)} %pos_ref.1) | copy-start | bytes 147460
  3.5 0.7 %copy-start.5 = (s32[2,32]{1,0:T(2,128)S(1)}, s32[2,32]{1,0:T(2,128)}, u32[]{:S(2)}) copy-start(s32[2,32]{1,0:T(2,128)} %sel_ref.3) | copy-start | bytes 772
  23.8 1.4 %copy-start = (bf16[128,6144]{1,0:T(8,128)(2,1)S(1)}, bf16[128,6144]{1,0:T(8,128)(2,1)}, u32[]{:S(2)}) copy-start(bf16[128,6144]{1,0:T(8,128)(2,1)} %q_ref.1) | copy-start | bytes 4718596
  25.2 0.9 %copy-start.2 = (bf16[128,768]{1,0:T(8,128)(2,1)S(1)}, bf16[128,768]{1,0:T(8,128)(2,1)}, u32[]{:S(2)}) copy-start(bf16[128,768]{1,0:T(8,128)(2,1)} %kv_ref.3) | copy-start | bytes 589828
  26.1 0.7 %copy-start.6 = (s32[2,32]{1,0:T(2,128)S(1)}, s32[2,32]{1,0:T(2,128)}, u32[]{:S(2)}) copy-start(s32[2,32]{1,0:T(2,128)} %sel_ref.3) | copy-start | bytes 772

commit v2 on v1

--- a/solution.py
+++ b/solution.py
@@ -19,19 +19,30 @@
 WIDE = 256
 CHUNK = 4
 PAIRS = GROUP_HEADS // 2
+SINK_ROWS = 64
+PARTS = 2
+PART_ROWS = GROUP_HEADS * BLOCK // PARTS
 NEG_FILL = -1e30
 EXP2_SCALE = HEAD_DIM ** (-0.5) * math.log2(math.e)
 FAR_POS = 1 << 30
 
 
-def exchange(grp_count, seq_count, kv_ref, sel_ref, pos_ref, map_ref, pool_ref, prev_ref, sums_ref,
-             lists, staged, mine, list_send, list_recv, data_send, data_recv, sum_send, sum_recv,
+def exchange(grp_count, seq_count, kv_in, sel_in, pos_in, map_in, pool_ref, prev_ref, sums_ref,
+             kv_ref, sel_ref, pos_ref, map_ref, load_sems, lists, staged, mine, list_send, list_recv, data_send, data_recv, sum_send, sum_recv,
              prev_send, prev_recv):
     grp = lax.axis_index("grp")
     seq = lax.axis_index("seq")
     last = seq_count - 1
     first_block = (grp * seq_count + seq) * 2
 
+    loads = [
+        pltpu.make_async_copy(src, dst, load_sems.at[i])
+        for i, (src, dst) in enumerate(
+            ((sel_in, sel_ref), (kv_in, kv_ref), (pos_in, pos_ref), (map_in, map_ref)))
+    ]
+    for load in loads:
+        load.start()
+
     barrier = pltpu.get_barrier_semaphore()
 
     def near(place):
@@ -69,6 +80,8 @@
 
     extra = tail_out.astype(jnp.int32) + tail_in.astype(jnp.int32)
     pl.semaphore_wait(barrier, seq_count + grp_count - 2 + extra)
+    for load in loads:
+        load.wait()
 
     def remote(src, dst, send, recv, where):
         return pltpu.make_async_remote_copy(
@@ -171,9 +184,14 @@
             jax.ShapeDtypeStruct(keys_values.shape, jnp.bfloat16),
             jax.ShapeDtypeStruct((seq_count, grp_count, 16, 128), jnp.bfloat16),
         ),
-        in_specs=[vmem] * 4,
+        in_specs=[pl.BlockSpec(memory_space=pl.ANY)] * 4,
         out_specs=(pl.BlockSpec(memory_space=pl.ANY), pl.BlockSpec(memory_space=pl.ANY), vmem),
         scratch_shapes=[
+            pltpu.VMEM(keys_values.shape, jnp.bfloat16),
+            pltpu.VMEM(selection.shape, jnp.int32),
+            pltpu.VMEM(pos_weight.shape, jnp.bfloat16),
+            pltpu.VMEM(compress_weight.shape, jnp.bfloat16),
+            pltpu.SemaphoreType.DMA((4,)),
             pltpu.VMEM((slots,) + selection.shape, jnp.int32),
             pltpu.VMEM((slots, BLOCK, GROUPS * PAIR), jnp.bfloat16),
             pltpu.VMEM((16, 128), jnp.bfloat16),
@@ -182,44 +200,32 @@
             pltpu.SemaphoreType.DMA,
         ],
         compiler_params=pltpu.CompilerParams(
-            collective_id=0, has_side_effects=True, vmem_limit_bytes=32 << 20),
+            collective_id=0, has_side_effects=True, vmem_limit_bytes=56 << 20),
     )(keys_values, selection, pos_weight, compress_weight)
 
 
-def spread(pair):
-    lane = lax.broadcasted_iota(jnp.int32, (pair.shape[0], WIDE), 1)
-    low = pair[:, 0:WIDE].astype(jnp.float32)
-    high = pair[:, PAIR - WIDE:PAIR].astype(jnp.float32)
-    key_even = jnp.where(lane < HEAD_DIM, low, 0.0)
-    key_odd = jnp.where(lane >= WIDE - HEAD_DIM, pltpu.roll(low, WIDE - HEAD_DIM, 1), 0.0)
-    value_even = jnp.where(lane < HEAD_DIM, pltpu.roll(high, HEAD_DIM, 1),
-                           jnp.where(lane == HEAD_DIM, 1.0, 0.0))
-    value_odd = jnp.where(lane >= WIDE - HEAD_DIM, high, jnp.where(lane == 0, 1.0, 0.0))
-    return [x.astype(jnp.bfloat16) for x in (key_even, key_odd, value_even, value_odd)]
-
-
-def branch(query_rows, keys, values, biases, with_sink, ones_lane):
+def value_rows(high):
+    lane = lax.broadcasted_iota(jnp.int32, high.shape, 1)
+    return jnp.where(lane >= WIDE - HEAD_DIM, high.astype(jnp.float32), 1.0).astype(jnp.bfloat16)
+
+
+def branch(query_rows, keys, values, biases):
     heads = query_rows.shape[0] // BLOCK
     scores = []
     for key, bias in zip(keys, biases):
         raw = lax.dot_general(query_rows, key, (((1,), (1,)), ((), ())), preferred_element_type=jnp.float32)
         scores.append((raw.reshape(heads, BLOCK, raw.shape[1]) + bias[None]).reshape(raw.shape))
-    top = functools.reduce(jnp.maximum, [jnp.max(s, axis=1, keepdims=True) for s in scores])
-    if with_sink:
-        top = jnp.maximum(top, 0.0)
+    top = jnp.max(functools.reduce(jnp.maximum, scores), axis=1, keepdims=True)
     total = None
     for score, value in zip(scores, values):
         weights = jnp.exp2((score - top) * EXP2_SCALE).astype(jnp.bfloat16)
         part = jnp.dot(weights, value, preferred_element_type=jnp.float32)
         total = part if total is None else total + part
-    below = total[:, ones_lane:ones_lane + 1]
-    if with_sink:
-        below = below + jnp.exp2(-top * EXP2_SCALE)
-    return total, below
+    return total
 
 
 def attend(grp_count, seq_count, sel_ref, q_ref, kv_ref, pool_ref, prev_ref, sums_ref, gate_ref,
-           out_ref, chosen, nearby, far_sums, acc, picks, spots):
+           out_ref, keys, values, near_keys, near_values, sums_keys, sums_values, rows, totals, picks, spots):
     slots = grp_count + seq_count
     grp = lax.axis_index("grp")
     seq = lax.axis_index("seq")
@@ -227,29 +233,40 @@
     b = pl.program_id(1)
     run = grp * seq_count + seq
     row_block = run * 2 + b
-    cols = pl.ds(pl.multiple_of(g * PAIR, 128), PAIR)
-    halves = PAIRS // 4
+    key_cols = pl.ds(pl.multiple_of(g * PAIR, 128), WIDE)
+    value_cols = pl.ds(pl.multiple_of(g * PAIR + PAIR - WIDE, 128), WIDE)
+    all_blocks = sums_ref.shape[1]
 
     @pl.when(b == 0)
     def _():
         def fill(slot, carry):
-            for i, x in enumerate(spread(pool_ref[slot, :, cols])):
-                chosen[i, slot] = x
+            keys[slot] = pool_ref[slot, :, key_cols]
+            values[slot] = value_rows(pool_ref[slot, :, value_cols])
             return carry
 
         lax.fori_loop(0, seq, fill, 0)
         lax.fori_loop(seq_count, seq_count + grp, fill, 0)
-        own = spread(kv_ref[:, cols])
-        before = spread(jnp.where(run > 0, prev_ref[:, cols], jnp.zeros_like(prev_ref[:, cols])))
-        for i in range(4):
-            chosen[i, slots] = own[i][0:BLOCK]
-            chosen[i, slots + 1] = own[i][BLOCK:2 * BLOCK]
-            nearby[i, 0:WINDOW] = before[i]
-            nearby[i, WINDOW:2 * WINDOW] = own[i]
-        for i, x in enumerate(spread(sums_ref[0])):
-            far_sums[i] = x
+        own = kv_ref[:, key_cols], value_rows(kv_ref[:, value_cols])
+        for i in range(2):
+            keys[slots + i] = own[0][i * BLOCK:(i + 1) * BLOCK]
+            values[slots + i] = own[1][i * BLOCK:(i + 1) * BLOCK]
+        before = prev_ref[:, key_cols]
+        near_keys[0:WINDOW] = jnp.where(run > 0, before, jnp.zeros_like(before))
+        before = value_rows(prev_ref[:, value_cols])
+        near_values[0:WINDOW] = jnp.where(run > 0, before, jnp.zeros_like(before))
+        near_keys[WINDOW:2 * WINDOW] = own[0]
+        near_values[WINDOW:2 * WINDOW] = own[1]
+        sums_keys[0:all_blocks] = sums_ref[0, :, 0:WIDE]
+        sums_values[0:all_blocks] = value_rows(sums_ref[0, :, PAIR - WIDE:PAIR])
+        pad = (SINK_ROWS, WIDE)
+        sums_keys[all_blocks:all_blocks + SINK_ROWS] = jnp.zeros(pad, jnp.bfloat16)
+        sums_values[all_blocks:all_blocks + SINK_ROWS] = value_rows(jnp.zeros(pad, jnp.bfloat16))
 
     seg_blocks = 2 * seq_count
+
+    for i in range(TOP):
+        picks[i] = slots + b
+        spots[i] = FAR_POS
 
     def scan(i, count):
         block = sel_ref[b, g * TOP + i]
@@ -265,19 +282,15 @@
 
         return count + jnp.where(block >= 0, 1, 0)
 
-    for i in range(TOP):
-        picks[i] = slots + b
-        spots[i] = FAR_POS
     count = lax.fori_loop(0, TOP, scan, jnp.int32(0))
 
-    @pl.when(count < TOP)
-    def _():
-        def blank(i, carry):
-            picks[i] = slots + b
-            spots[i] = FAR_POS
-            return carry
-
-        lax.fori_loop(count, TOP, blank, 0)
+    wide_lane = lax.broadcasted_iota(jnp.int32, (BLOCK, WIDE), 1)
+    for h in range(GROUP_HEADS):
+        start = (h // 2) * PAIR + (h % 2) * (PAIR - WIDE)
+        part = q_ref[:, start:start + WIDE].astype(jnp.float32)
+        if h % 2:
+            part = pltpu.roll(part, HEAD_DIM, 1)
+        rows[h * BLOCK:(h + 1) * BLOCK] = jnp.where(wide_lane < HEAD_DIM, part, 0.0).astype(jnp.bfloat16)
 
     token = row_block * BLOCK + lax.broadcasted_iota(jnp.int32, (BLOCK, 1), 0)
 
@@ -286,36 +299,16 @@
 
     key_pos = run * 2 * BLOCK - WINDOW + lax.broadcasted_iota(jnp.int32, (BLOCK, 2 * WINDOW), 1)
     near_bias = bias_of((key_pos <= token) & (key_pos > token - WINDOW) & (key_pos >= 0))
-    all_blocks = sums_ref.shape[1]
-    block_end = lax.broadcasted_iota(jnp.int32, (BLOCK, all_blocks), 1) * BLOCK + BLOCK - 1
-    sums_bias = bias_of(block_end <= token)
-
-    gates = []
-    for i in range(3):
-        full = 1.0 / (1.0 + jnp.exp(-gate_ref[i].astype(jnp.float32)))
-        gates.append(jnp.where(g == 0, full[:, 0:GROUP_HEADS], full[:, GROUP_HEADS:HEADS]))
-
-    def rows_of(half, parity):
-        starts = [(half * 4 + j) * PAIR + parity * (PAIR - WIDE) for j in range(4)]
-        return jnp.concatenate([q_ref[:, s:s + WIDE] for s in starts], axis=0)
-
-    def gate_of(i, half, parity):
-        heads = [2 * (half * 4 + j) + parity for j in range(4)]
-        return jnp.concatenate([gates[i][:, h:h + 1] for h in heads], axis=0)
-
-    ones_lane = (HEAD_DIM, 0)
-    for half in range(halves):
-        for parity in range(2):
-            rows = rows_of(half, parity)
-            near_total, near_below = branch(
-                rows, [nearby[parity]], [nearby[2 + parity]], [near_bias], False, ones_lane[parity])
-            sums_total, sums_below = branch(
-                rows, [far_sums[parity]], [far_sums[2 + parity]], [sums_bias], True, ones_lane[parity])
-            acc[half, parity] = (near_total * (gate_of(2, half, parity) / near_below)
-                                 + sums_total * (gate_of(0, half, parity) / sums_below))
+    block_id = lax.broadcasted_iota(jnp.int32, (BLOCK, all_blocks + SINK_ROWS), 1)
+    sums_bias = bias_of(((block_id < all_blocks) & (block_id * BLOCK + BLOCK - 1 <= token))
+                        | (block_id == all_blocks))
+
+    for part in range(PARTS):
+        at = slice(part * PART_ROWS, (part + 1) * PART_ROWS)
+        totals[0, at] = branch(rows[at], [sums_keys[...]], [sums_values[...]], [sums_bias])
+        totals[2, at] = branch(rows[at], [near_keys[...]], [near_values[...]], [near_bias])
 
     lane = lax.broadcasted_iota(jnp.int32, (BLOCK, CHUNK * BLOCK), 1)
-    half_lane = lax.broadcasted_iota(jnp.int32, (BLOCK, 128), 1) < 64
 
     def selected(chunks):
         biases = []
@@ -324,26 +317,16 @@
             for j in range(1, CHUNK):
                 base = jnp.where(lane >= j * BLOCK, spots[c * CHUNK + j], base)
             biases.append(bias_of(base + (lane & (BLOCK - 1)) <= token))
-        for half in range(halves):
-            both = []
-            for parity in range(2):
-                def take(which):
-                    return [
-                        jnp.concatenate([chosen[which, picks[c * CHUNK + j]] for j in range(CHUNK)], axis=0)
-                        for c in range(chunks)
-                    ]
-
-                total, below = branch(
-                    rows_of(half, parity), take(parity), take(2 + parity), biases, False, ones_lane[parity])
-                both.append(acc[half, parity] + total * (gate_of(1, half, parity) / below))
-            for j in range(4):
-                even = both[0][j * BLOCK:(j + 1) * BLOCK]
-                odd = both[1][j * BLOCK:(j + 1) * BLOCK]
-                start = (half * 4 + j) * PAIR
-                out_ref[:, start:start + 128] = even[:, 0:128].astype(jnp.bfloat16)
-                out_ref[:, start + 128:start + 256] = jnp.where(
-                    half_lane, even[:, 128:256], odd[:, 0:128]).astype(jnp.bfloat16)
-                out_ref[:, start + 256:start + 384] = odd[:, 128:256].astype(jnp.bfloat16)
+
+        def take(ref):
+            return [
+                jnp.concatenate([ref[picks[c * CHUNK + j]] for j in range(CHUNK)], axis=0)
+                for c in range(chunks)
+            ]
+
+        for part in range(PARTS):
+            at = slice(part * PART_ROWS, (part + 1) * PART_ROWS)
+            totals[1, at] = branch(rows[at], take(keys), take(values), biases)
 
     for chunks in range(1, TOP // CHUNK + 1):
         low = 0 if chunks == 1 else (chunks - 1) * CHUNK + 1
@@ -351,6 +334,31 @@
         @pl.when(jnp.logical_and(count >= low, count <= chunks * CHUNK))
         def _():
             selected(chunks)
+
+    head_lane = lax.broadcasted_iota(jnp.int32, (BLOCK, HEADS), 1)
+    ratios = []
+    for i in range(3):
+        below = jnp.ones((BLOCK, HEADS), jnp.float32)
+        for h in range(GROUP_HEADS):
+            below = jnp.where(head_lane == g * GROUP_HEADS + h, totals[i, h * BLOCK:(h + 1) * BLOCK, 0:HEADS], below)
+        gate = 1.0 / (1.0 + jnp.exp(-gate_ref[i].astype(jnp.float32)))
+        ratio = gate / below
+        ratios.append(jnp.where(g == 0, ratio[:, 0:GROUP_HEADS], ratio[:, GROUP_HEADS:HEADS]))
+
+    half_lane = lax.broadcasted_iota(jnp.int32, (BLOCK, 128), 1) < 64
+
+    def mixed(h):
+        at = slice(h * BLOCK, (h + 1) * BLOCK)
+        return sum(totals[i, at] * ratios[i][:, h:h + 1] for i in range(3))
+
+    for j in range(PAIRS):
+        even = pltpu.roll(mixed(2 * j), HEAD_DIM, 1)
+        odd = mixed(2 * j + 1)
+        start = j * PAIR
+        out_ref[:, start:start + 128] = even[:, 0:128].astype(jnp.bfloat16)
+        out_ref[:, start + 128:start + 256] = jnp.where(
+            half_lane, even[:, 128:256], odd[:, 0:128]).astype(jnp.bfloat16)
+        out_ref[:, start + 256:start + 384] = odd[:, 128:256].astype(jnp.bfloat16)
 
 
 def run_attend(selection, queries, keys_values, pool, prev, sums, gate_logits):
@@ -377,15 +385,19 @@
             ],
             out_specs=pl.BlockSpec((BLOCK, group_cols), lambda g, b, *_: (b, g)),
             scratch_shapes=[
-                pltpu.VMEM((4, slots + 2, BLOCK, WIDE), jnp.bfloat16),
-                pltpu.VMEM((4, 2 * WINDOW, WIDE), jnp.bfloat16),
-                pltpu.VMEM((4, all_blocks, WIDE), jnp.bfloat16),
-                pltpu.VMEM((PAIRS // 4, 2, 4 * BLOCK, WIDE), jnp.float32),
+                pltpu.VMEM((slots + 2, BLOCK, WIDE), jnp.bfloat16),
+                pltpu.VMEM((slots + 2, BLOCK, WIDE), jnp.bfloat16),
+                pltpu.VMEM((2 * WINDOW, WIDE), jnp.bfloat16),
+                pltpu.VMEM((2 * WINDOW, WIDE), jnp.bfloat16),
+                pltpu.VMEM((all_blocks + SINK_ROWS, WIDE), jnp.bfloat16),
+                pltpu.VMEM((all_blocks + SINK_ROWS, WIDE), jnp.bfloat16),
+                pltpu.VMEM((GROUP_HEADS * BLOCK, WIDE), jnp.bfloat16),
+                pltpu.VMEM((3, GROUP_HEADS * BLOCK, WIDE), jnp.float32),
                 pltpu.SMEM((TOP,), jnp.int32),
                 pltpu.SMEM((TOP,), jnp.int32),
             ],
         ),
-        compiler_params=pltpu.CompilerParams(vmem_limit_bytes=48 << 20),
+        compiler_params=pltpu.CompilerParams(vmem_limit_bytes=56 << 20),
     )(selection, queries, keys_values, pool, prev, sums, gate_logits)
 
 

time: 50.7 us -> 42.1 us (0.83)
  Pallas kernels: 42.8 us -> 38.4 us
  local copies, waits for them, and re-layouts: 7.44 us -> 3.25 us
    unnamed x15 -> x1, local copies, waits for them, and re-layouts: 7.22 us -> 1.47 us
    pallas_call x1, Pallas kernels: 23.5 us -> 18.4 us  [run_attend(): pl.pallas_call(functools.partial(attend, grp_count, seq_count), out_shape...]
    slice x1, local copies, waits for them, and re-layouts: 0.07 us -> 0.97 us  [shards(): sums = packed[:, :, :12].reshape(seq_count, grp_count, 3, 2, GROUPS, 128)]
    pallas_call x1, Pallas kernels: 19.3 us -> 20 us  [run_exchange(): pl.pallas_call(functools.partial(exchange, grp_count, seq_count), out_sha...]
    reshape x1, local copies, waits for them, and re-layouts: 0.08 us -> 0.73 us  [shards(): jnp.transpose(sums, (4, 1, 0, 3, 2, 5))]
where the time goes in v2:
time: 42.1 us; the launch traced here: 41.6 us
  Pallas kernels  38.4 us (91%)
  local copies, waits for them, and re-layouts  3.25 us (8%)
    pallas_call x1, Pallas kernels, run_exchange(): pl.pallas_call(functools.partial(exchange, grp_count, seq_count), out_sha...  20 us
    pallas_call x1, Pallas kernels, run_attend(): pl.pallas_call(functools.partial(attend, grp_count, seq_count), out_shape...  18.4 us
    unnamed x1, local copies, waits for them, and re-layouts  1.47 us
    slice x1, local copies, waits for them, and re-layouts, shards(): sums = packed[:, :, :12].reshape(seq_count, grp_count, 3, 2, GROUPS, 128)  0.97 us

profile of v2, /device:TPU:7, one launch (start us, length us, event | category | flops | bytes accessed | tf_op | source)
XLA Modules:
  0.0 41.6 jit_solution(5761543342634793466)
XLA Ops:
  0.0 1.5 %copy.11.gate_ref = bf16[3,128,32]{2,1,0:T(8,128)(2,1)} copy(bf16[3,128,32]{1,2,0:T(8,128)(2,1)} %param.9) | data formatting | bytes 49152 | tf_op args[3]
  1.5 20.0 %shard_map.64 = (bf16[12,64,768]{2,1,0:T(8,128)(2,1)}, bf16[128,768]{1,0:T(8,128)(2,1)}, bf16[8,4,16,128]{3,2,1,0:T(8,128)(2,1)}) custom-call(bf16[128,768]{1,0:T(8,128)(2,1)} %kv_ref.1, s32[2,32]{1,0:T(2,128)} %sel_ref.1, bf16[64,384]{1,0:T(8,128)(2,1)} %pos_in.1, bf16[384,384]{1,0:T(8,128)(2,1)} %map_in.1), custom_call_target="tpu_custom_call" | custom-call | tf_op jit(solution)/shard_map/pallas_call | solution.py:180
  21.5 1.0 %copy.9 = bf16[8,4,12,128]{3,0,2,1:T(8,128)(2,1)S(1)} copy(bf16[8,4,12,128]{3,2,1,0:T(8,128)(2,1)} %bitcast.5) | data formatting | bytes 196608 | tf_op jit(solution)/shard_map/slice | solution.py:408
  22.4 0.1 copy.10
  22.5 0.7 %reshape.7.sums_ref = bf16[2,64,384]{2,1,0:T(8,128)(2,1)} reshape(bf16[2,4,8,2,3,128]{5,4,3,2,1,0:T(4,128)(2,1)S(1)} %copy.10) | data formatting | bytes 196608 | tf_op jit(solution)/shard_map/reshape | solution.py:409
  23.2 18.4 %shard_map.65 = bf16[128,6144]{1,0:T(8,128)(2,1)} custom-call(s32[2,32]{1,0:T(2,128)} %sel_ref.1, bf16[128,6144]{1,0:T(8,128)(2,1)} %q_ref.1, bf16[128,768]{1,0:T(8,128)(2,1)} %kv_ref.1, bf16[12,64,768]{2,1,0:T(8,128)(2,1)} %get-tuple-element.8.pool_ref, bf16[128,768]{1,0:T(8,128)(2,1)} %get-tuple-element.9.prev_ref, bf16[2,64,384]{2,1,0:T(8,128)(2,1)} %reshape.7.sums_ref, ...), custom_call_target="tpu_custom_call" | custom-call | tf_op jit(solution)/shard_map/pallas_call | solution.py:374

commit v3 on v2

--- a/solution.py
+++ b/solution.py
@@ -92,7 +92,7 @@
         return remote(sel_ref, lists.at[own], list_send.at[theirs], list_recv.at[own], where)
 
     each(0, grp, lambda i: list_copy(seq_count + i, seq_count + grp, far(i)).start())
-    each(0, seq, lambda i: list_copy(i, seq, near(i)).start())
+    each(0, seq - 1, lambda i: list_copy(i, seq, near(i)).start())
 
     def prev_copy(where):
         return remote(kv_ref, prev_ref, prev_send, prev_recv, where)
@@ -138,7 +138,7 @@
         data_copy(slot, own, where).start()
 
     each(grp + 1, grp_count, lambda i: answer(seq_count + i, seq_count + grp, far(i)))
-    each(seq + 1, seq_count, lambda i: answer(i, seq, near(i)))
+    each(seq + 2, seq_count, lambda i: answer(i, seq, near(i)))
 
     others(grp_count, grp, lambda i: column_copy(seq_count + i, seq_count + i, far(i)).wait_recv())
 
@@ -153,7 +153,7 @@
     others(seq_count, seq, row_wait)
 
     each(0, grp, lambda i: data_copy(seq_count + i, seq_count + i, far(i)).wait_recv())
-    each(0, seq, lambda i: data_copy(i, i, near(i)).wait_recv())
+    each(0, seq - 1, lambda i: data_copy(i, i, near(i)).wait_recv())
 
     @pl.when(jnp.logical_or(seq > 0, grp > 0))
     def _():
@@ -164,9 +164,9 @@
         prev_copy(far(grp)).wait_send()
 
     each(0, grp, lambda i: list_copy(seq_count + i, seq_count + i, far(i)).wait_send())
-    each(0, seq, lambda i: list_copy(i, i, near(i)).wait_send())
+    each(0, seq - 1, lambda i: list_copy(i, i, near(i)).wait_send())
     each(grp + 1, grp_count, lambda i: data_copy(seq_count + i, seq_count + i, far(i)).wait_send())
-    each(seq + 1, seq_count, lambda i: data_copy(i, i, near(i)).wait_send())
+    each(seq + 2, seq_count, lambda i: data_copy(i, i, near(i)).wait_send())
     others(grp_count, grp, lambda i: column_copy(seq_count + i, seq_count + i, far(i)).wait_send())
     others(seq_count, seq, lambda i: row_copy(i, seq, near(i)).wait_send())
 
@@ -225,7 +225,8 @@
 
 
 def attend(grp_count, seq_count, sel_ref, q_ref, kv_ref, pool_ref, prev_ref, sums_ref, gate_ref,
-           out_ref, keys, values, near_keys, near_values, sums_keys, sums_values, rows, totals, picks, spots):
+           out_ref, keys, values, near_keys, near_values, sums_keys, sums_values, rows, totals,
+           unpacked, opened, picks, spots):
     slots = grp_count + seq_count
     grp = lax.axis_index("grp")
     seq = lax.axis_index("seq")
@@ -235,7 +236,13 @@
     row_block = run * 2 + b
     key_cols = pl.ds(pl.multiple_of(g * PAIR, 128), WIDE)
     value_cols = pl.ds(pl.multiple_of(g * PAIR + PAIR - WIDE, 128), WIDE)
-    all_blocks = sums_ref.shape[1]
+    runs = grp_count * seq_count
+    all_blocks = 2 * runs
+
+    @pl.when(jnp.logical_and(g == 0, b == 0))
+    def _():
+        for i in range(3):
+            opened[i] = (1.0 / (1.0 + jnp.exp(-gate_ref[i].astype(jnp.float32)))).T
 
     @pl.when(b == 0)
     def _():
@@ -244,20 +251,32 @@
             values[slot] = value_rows(pool_ref[slot, :, value_cols])
             return carry
 
-        lax.fori_loop(0, seq, fill, 0)
+        lax.fori_loop(0, seq - 1, fill, 0)
         lax.fori_loop(seq_count, seq_count + grp, fill, 0)
         own = kv_ref[:, key_cols], value_rows(kv_ref[:, value_cols])
         for i in range(2):
             keys[slots + i] = own[0][i * BLOCK:(i + 1) * BLOCK]
             values[slots + i] = own[1][i * BLOCK:(i + 1) * BLOCK]
         before = prev_ref[:, key_cols]
-        near_keys[0:WINDOW] = jnp.where(run > 0, before, jnp.zeros_like(before))
-        before = value_rows(prev_ref[:, value_cols])
-        near_values[0:WINDOW] = jnp.where(run > 0, before, jnp.zeros_like(before))
+        before = jnp.where(run > 0, before, jnp.zeros_like(before))
+        near_keys[0:WINDOW] = before
+        after = value_rows(prev_ref[:, value_cols])
+        after = jnp.where(run > 0, after, jnp.zeros_like(after))
+        near_values[0:WINDOW] = after
+        for i in range(2):
+            keys[slots + 2 + i] = before[i * BLOCK:(i + 1) * BLOCK]
+            values[slots + 2 + i] = after[i * BLOCK:(i + 1) * BLOCK]
         near_keys[WINDOW:2 * WINDOW] = own[0]
         near_values[WINDOW:2 * WINDOW] = own[1]
-        sums_keys[0:all_blocks] = sums_ref[0, :, 0:WIDE]
-        sums_values[0:all_blocks] = value_rows(sums_ref[0, :, PAIR - WIDE:PAIR])
+        unpacked[...] = sums_ref[...].reshape(runs * 16, 128).astype(jnp.float32)
+        for half in range(2):
+            thirds = [
+                unpacked[pl.ds(c * 4 + half * GROUPS + g, runs, stride=16), :].astype(jnp.bfloat16)
+                for c in range(3)
+            ]
+            at = slice(half * runs, (half + 1) * runs)
+            sums_keys[at] = jnp.concatenate(thirds[0:2], axis=1)
+            sums_values[at] = value_rows(jnp.concatenate(thirds[1:3], axis=1))
         pad = (SINK_ROWS, WIDE)
         sums_keys[all_blocks:all_blocks + SINK_ROWS] = jnp.zeros(pad, jnp.bfloat16)
         sums_values[all_blocks:all_blocks + SINK_ROWS] = value_rows(jnp.zeros(pad, jnp.bfloat16))
@@ -274,6 +293,8 @@
         place = (block - segment * seg_blocks) // 2
         here = jnp.logical_and(segment == grp, place == seq)
         slot = jnp.where(here, slots + (block & 1), jnp.where(segment == grp, place, seq_count + segment))
+        just_before = jnp.logical_and(segment == grp, place == seq - 1)
+        slot = jnp.where(just_before, slots + 2 + (block & 1), slot)
 
         @pl.when(block >= 0)
         def _():
@@ -299,9 +320,13 @@
 
     key_pos = run * 2 * BLOCK - WINDOW + lax.broadcasted_iota(jnp.int32, (BLOCK, 2 * WINDOW), 1)
     near_bias = bias_of((key_pos <= token) & (key_pos > token - WINDOW) & (key_pos >= 0))
-    block_id = lax.broadcasted_iota(jnp.int32, (BLOCK, all_blocks + SINK_ROWS), 1)
-    sums_bias = bias_of(((block_id < all_blocks) & (block_id * BLOCK + BLOCK - 1 <= token))
-                        | (block_id == all_blocks))
+    column = lax.broadcasted_iota(jnp.int32, (BLOCK, all_blocks + SINK_ROWS), 1)
+    half = jnp.where(column >= runs, 1, 0)
+    member = column - half * runs
+    place = member // grp_count
+    block_id = ((member - place * grp_count) * seq_count + place) * 2 + half
+    sums_bias = bias_of(((column < all_blocks) & (block_id * BLOCK + BLOCK - 1 <= token))
+                        | (column == all_blocks))
 
     for part in range(PARTS):
         at = slice(part * PART_ROWS, (part + 1) * PART_ROWS)
@@ -341,8 +366,7 @@
         below = jnp.ones((BLOCK, HEADS), jnp.float32)
         for h in range(GROUP_HEADS):
             below = jnp.where(head_lane == g * GROUP_HEADS + h, totals[i, h * BLOCK:(h + 1) * BLOCK, 0:HEADS], below)
-        gate = 1.0 / (1.0 + jnp.exp(-gate_ref[i].astype(jnp.float32)))
-        ratio = gate / below
+        ratio = opened[i, pl.ds(pl.multiple_of(b * BLOCK, BLOCK), BLOCK)] / below
         ratios.append(jnp.where(g == 0, ratio[:, 0:GROUP_HEADS], ratio[:, GROUP_HEADS:HEADS]))
 
     half_lane = lax.broadcasted_iota(jnp.int32, (BLOCK, 128), 1) < 64
@@ -365,7 +389,7 @@
     grp_count = lax.axis_size("grp")
     seq_count = lax.axis_size("seq")
     slots = grp_count + seq_count
-    all_blocks = sums.shape[1]
+    all_blocks = 2 * grp_count * seq_count
 
     def whole(x):
         return pl.BlockSpec(x.shape, lambda g, b, *_: (0,) * x.ndim)
@@ -380,19 +404,21 @@
             in_specs=[
                 pl.BlockSpec((BLOCK, group_cols), lambda g, b, *_: (b, g)),
                 whole(keys_values), whole(pool), whole(prev),
-                pl.BlockSpec((1, all_blocks, PAIR), lambda g, b, *_: (g, 0, 0)),
-                pl.BlockSpec((3, BLOCK, HEADS), lambda g, b, *_: (0, b, 0)),
+                whole(sums),
+                whole(gate_logits),
             ],
             out_specs=pl.BlockSpec((BLOCK, group_cols), lambda g, b, *_: (b, g)),
             scratch_shapes=[
-                pltpu.VMEM((slots + 2, BLOCK, WIDE), jnp.bfloat16),
-                pltpu.VMEM((slots + 2, BLOCK, WIDE), jnp.bfloat16),
+                pltpu.VMEM((slots + 4, BLOCK, WIDE), jnp.bfloat16),
+                pltpu.VMEM((slots + 4, BLOCK, WIDE), jnp.bfloat16),
                 pltpu.VMEM((2 * WINDOW, WIDE), jnp.bfloat16),
                 pltpu.VMEM((2 * WINDOW, WIDE), jnp.bfloat16),
                 pltpu.VMEM((all_blocks + SINK_ROWS, WIDE), jnp.bfloat16),
                 pltpu.VMEM((all_blocks + SINK_ROWS, WIDE), jnp.bfloat16),
                 pltpu.VMEM((GROUP_HEADS * BLOCK, WIDE), jnp.bfloat16),
                 pltpu.VMEM((3, GROUP_HEADS * BLOCK, WIDE), jnp.float32),
+                pltpu.VMEM((all_blocks * 8, 128), jnp.float32),
+                pltpu.VMEM((3, 2 * BLOCK, HEADS), jnp.float32),
                 pltpu.SMEM((TOP,), jnp.int32),
                 pltpu.SMEM((TOP,), jnp.int32),
             ],
@@ -402,12 +428,9 @@
 
 
 def shards(queries, keys_values, selection, gate_logits, pos_weight, compress_weight):
-    grp_count = lax.axis_size("grp")
-    seq_count = lax.axis_size("seq")
     pool, prev, packed = run_exchange(keys_values, selection, pos_weight, compress_weight)
-    sums = packed[:, :, :12].reshape(seq_count, grp_count, 3, 2, GROUPS, 128)
-    sums = jnp.transpose(sums, (4, 1, 0, 3, 2, 5)).reshape(GROUPS, 2 * seq_count * grp_count, PAIR)
-    return run_attend(selection, queries, keys_values, pool, prev, sums, gate_logits)
+    return run_attend(
+        selection, queries, keys_values, pool, prev, packed, jnp.transpose(gate_logits, (0, 2, 1)))
 
 
 def solution(mesh):

time: 42.1 us -> 38.5 us (0.914)
  local copies, waits for them, and re-layouts: 3.25 us -> 0 us
    unnamed x1 -> x0, local copies, waits for them, and re-layouts: 1.47 us -> none
    slice x1 -> x0, local copies, waits for them, and re-layouts: 0.97 us -> none  [shards(): sums = packed[:, :, :12].reshape(seq_count, grp_count, 3, 2, GROUPS, 128)]
    reshape x1 -> x0, local copies, waits for them, and re-layouts: 0.73 us -> none  [shards(): jnp.transpose(sums, (4, 1, 0, 3, 2, 5))]
where the time goes in v3:
time: 38.5 us; the launch traced here: 38.3 us
  Pallas kernels  38.2 us (99%)
    pallas_call x1, Pallas kernels, run_exchange(): pl.pallas_call(functools.partial(exchange, grp_count, seq_count), out_sha...  19.8 us
    pallas_call x1, Pallas kernels, run_attend(): pl.pallas_call(functools.partial(attend, grp_count, seq_count), out_shape...  18.4 us

profile of v3, /device:TPU:7, one launch (start us, length us, event | category | flops | bytes accessed | tf_op | source)
XLA Modules:
  0.0 38.3 jit_solution(8743067883494067891)
XLA Ops:
  0.0 19.8 %shard_map.64 = (bf16[12,64,768]{2,1,0:T(8,128)(2,1)}, bf16[128,768]{1,0:T(8,128)(2,1)}, bf16[8,4,16,128]{3,2,1,0:T(8,128)(2,1)}) custom-call(bf16[128,768]{1,0:T(8,128)(2,1)} %kv_ref.1, s32[2,32]{1,0:T(2,128)} %sel_ref.1, bf16[64,384]{1,0:T(8,128)(2,1)} %pos_in.1, bf16[384,384]{1,0:T(8,128)(2,1)} %map_in.1), custom_call_target="tpu_custom_call" | custom-call | tf_op jit(solution)/shard_map/pallas_call | solution.py:180
  19.9 18.4 %shard_map.65 = bf16[128,6144]{1,0:T(8,128)(2,1)} custom-call(s32[2,32]{1,0:T(2,128)} %sel_ref.1, bf16[128,6144]{1,0:T(8,128)(2,1)} %q_ref.1, bf16[128,768]{1,0:T(8,128)(2,1)} %kv_ref.1, bf16[12,64,768]{2,1,0:T(8,128)(2,1)} %get-tuple-element.8.pool_ref, bf16[128,768]{1,0:T(8,128)(2,1)} %get-tuple-element.9.prev_ref, ...), custom_call_target="tpu_custom_call" | custom-call | tf_op jit(solution)/shard_map/pallas_call | solution.py:398

commit v4 on v3

--- a/solution.py
+++ b/solution.py
@@ -371,9 +371,22 @@
 
     half_lane = lax.broadcasted_iota(jnp.int32, (BLOCK, 128), 1) < 64
 
+    stacked = jnp.concatenate(ratios, axis=0)
+    coarse = stacked.astype(jnp.bfloat16)
+    fine = (stacked - coarse.astype(jnp.float32)).astype(jnp.bfloat16)
+    source = lax.broadcasted_iota(jnp.int32, (GROUP_HEADS, GROUP_HEADS * 128), 0)
+    target = lax.broadcasted_iota(jnp.int32, (GROUP_HEADS, GROUP_HEADS * 128), 1) // 128
+    pattern = jnp.where(source == target, 1.0, 0.0).astype(jnp.bfloat16)
+    spread = (jnp.dot(coarse, pattern, preferred_element_type=jnp.float32)
+              + jnp.dot(fine, pattern, preferred_element_type=jnp.float32))
+
     def mixed(h):
         at = slice(h * BLOCK, (h + 1) * BLOCK)
-        return sum(totals[i, at] * ratios[i][:, h:h + 1] for i in range(3))
+        sides = [
+            sum(totals[i, at, s:s + 128] * spread[i * BLOCK:(i + 1) * BLOCK, h * 128:(h + 1) * 128] for i in range(3))
+            for s in (0, 128)
+        ]
+        return jnp.concatenate(sides, axis=1)
 
     for j in range(PAIRS):
         even = pltpu.roll(mixed(2 * j), HEAD_DIM, 1)

time: 38.5 us -> 37.3 us (0.969)
  Pallas kernels: 38.2 us -> 37 us
    pallas_call x1, Pallas kernels: 18.4 us -> 17.1 us  [run_attend(): pl.pallas_call(functools.partial(attend, grp_count, seq_count), out_shape...]
where the time goes in v4:
time: 37.3 us; the launch traced here: 37 us
  Pallas kernels  37 us (99%)
    pallas_call x1, Pallas kernels, run_exchange(): pl.pallas_call(functools.partial(exchange, grp_count, seq_count), out_sha...  19.8 us
    pallas_call x1, Pallas kernels, run_attend(): pl.pallas_call(functools.partial(attend, grp_count, seq_count), out_shape...  17.1 us

profile of v4, /device:TPU:7, one launch (start us, length us, event | category | flops | bytes accessed | tf_op | source)
XLA Modules:
  0.0 37.0 jit_solution(12886105944540353046)
XLA Ops:
  0.0 19.8 %shard_map.64 = (bf16[12,64,768]{2,1,0:T(8,128)(2,1)}, bf16[128,768]{1,0:T(8,128)(2,1)}, bf16[8,4,16,128]{3,2,1,0:T(8,128)(2,1)}) custom-call(bf16[128,768]{1,0:T(8,128)(2,1)} %kv_ref.1, s32[2,32]{1,0:T(2,128)} %sel_ref.1, bf16[64,384]{1,0:T(8,128)(2,1)} %pos_in.1, bf16[384,384]{1,0:T(8,128)(2,1)} %map_in.1), custom_call_target="tpu_custom_call" | custom-call | tf_op jit(solution)/shard_map/pallas_call | solution.py:180
  19.9 17.1 %shard_map.65 = bf16[128,6144]{1,0:T(8,128)(2,1)} custom-call(s32[2,32]{1,0:T(2,128)} %sel_ref.1, bf16[128,6144]{1,0:T(8,128)(2,1)} %q_ref.1, bf16[128,768]{1,0:T(8,128)(2,1)} %kv_ref.1, bf16[12,64,768]{2,1,0:T(8,128)(2,1)} %get-tuple-element.8.pool_ref, bf16[128,768]{1,0:T(8,128)(2,1)} %get-tuple-element.9.prev_ref, ...), custom_call_target="tpu_custom_call" | custom-call | tf_op jit(solution)/shard_map/pallas_call | solution.py:411
